TPU v7x, 512 devices: a whole 4x4x16 slice. The times are simulated.
512 devices in a mesh: mn: 32 (over y, z_hi, x), az: 16 (over z_lo, core).
Axes of the slice: x: 4, y: 4, z: 16 (z_hi: 2, z_lo: 8; z = z_hi * 8 + z_lo), core: 2. Of those that a mesh axis runs over, the one named last changes fastest.
Arguments:
- flow_state: float32 [41, 256, 128, 128], P(None, 'mn', 'az'), may hold values from -12 to 12, as said below
- level_rates: float32 [30, 30], replicated, may hold values from -0.6 to 0.6
Outputs:
- new_state: float32 [41, 256, 128, 128], P(None, 'mn', 'az')
Inputs may be any that keep to these rules, and one draw needn't show every extreme that they name: `flow_state`: quantities 0 to 4 lie in 0.05 to 0.45 and quantity 10 in 0.5 to 2.
All inputs are finite; a program needn't handle non-finite values.
Results may differ from a plain program's by a relative error of at most 0.000098.
Values sent between devices are 32-bit elements; how exact they have to be, the bound alone decides.
A program may use at most 64 MiB of HBM per device.

v0:
```python
import jax
import jax.numpy as jnp
from jax import lax
from jax.sharding import PartitionSpec as P

DISSIPATION = 0.05
SOUND_SPEED = 1.0
TIME_STEP = 0.3


def with_halo(value, sides, width, wrap):
    for axis, dim in sides:
        size, length = (lax.axis_size(axis), value.shape[dim])
        up = [(i, (i + 1) % size) for i in range(size if wrap else size - 1)]
        down = [(j, i) for i, j in up]
        last = lax.slice_in_dim(value, length - width, length, axis=dim)
        first = lax.slice_in_dim(value, 0, width, axis=dim)
        before = lax.ppermute(last, axis, up)
        after = lax.ppermute(first, axis, down)
        value = jnp.concatenate([before, value, after], axis=dim)
    return value


def from_behind(block, axis, distance):
    devices = range(lax.axis_size(axis))
    route = [((i - distance) % len(devices), i) for i in devices]
    return lax.ppermute(block, axis, route)


def pole_sign(count):
    position = jnp.arange(count)
    return jnp.where((position == 5) | (position == 7), -1.0, 1.0).astype(jnp.float32)[
        :, None, None, None
    ]


def face_div(fields, velocity, axis, count):

    def window(array, offset):
        return lax.slice_in_dim(array, offset, offset + count + 1, axis=axis)

    carried = velocity * fields
    wave_speed = 0.5 * (jnp.abs(window(velocity, 1)) + jnp.abs(window(velocity, 2))) + SOUND_SPEED
    fourth = (
        window(fields, 3) - 3.0 * window(fields, 2) + 3.0 * window(fields, 1) - window(fields, 0)
    )
    flux = 0.5 * (window(carried, 1) + window(carried, 2)) - DISSIPATION * wave_speed * fourth
    return lax.slice_in_dim(flux, 1, count + 1, axis=axis) - lax.slice_in_dim(
        flux, 0, count, axis=axis
    )


def velocity_of(padded):
    density = jnp.sum(padded[0:5], axis=0, keepdims=True)
    return padded[5:8] / jnp.maximum(density, 1.0)


def residual(padded, velocity, level_rates):
    inner_i = padded.shape[1] - 4
    inner_k = padded.shape[2] - 4
    along_i = face_div(padded[:, :, 2:-2], velocity[0:1, :, 2:-2], 1, inner_i)
    along_k = face_div(padded[:, 2:-2], velocity[2:3, 2:-2], 2, inner_k)
    centre = padded[:, 2:-2, 2:-2]
    widths = ((0, 0), (0, 0), (0, 0), (2, 2))
    along_j = face_div(
        jnp.pad(centre, widths), jnp.pad(velocity[1:2, 2:-2, 2:-2], widths), 3, centre.shape[3]
    )
    change = -(along_i + along_k + along_j)
    source = centre[10:11] * jnp.einsum(
        "ab,bikj->aikj", level_rates, centre[11:], precision=lax.Precision.HIGHEST
    )
    return jnp.concatenate([change[:11], change[11:] + source], axis=0)


def azimuth_ghosts(fields):
    return with_halo(fields, (("az", 2),), 2, True)


def pole_rows(fields):
    return fields[:, 0:2][:, ::-1] * pole_sign(fields.shape[0])


def join_pole(opposite, padded):
    at_pole = lax.axis_index("mn") == 0
    lower = jnp.where(at_pole, opposite, padded[:, 0:2])
    return jnp.concatenate([lower, padded[:, 2:]], axis=1)


def meridian_ghosts(fields):
    opposite = from_behind(pole_rows(fields), "az", lax.axis_size("az") // 2)
    padded = with_halo(fields, (("mn", 1),), 2, False)
    return join_pole(opposite, padded)


def on_device(flow_state, level_rates):
    ghosted = meridian_ghosts(azimuth_ghosts(flow_state))
    velocity = velocity_of(ghosted)
    section_one = flow_state + TIME_STEP * residual(ghosted, velocity, level_rates)
    second = residual(meridian_ghosts(azimuth_ghosts(section_one)), velocity, level_rates)
    return 0.5 * flow_state + 0.5 * (section_one + TIME_STEP * second)


def solution(mesh):
    in_specs = (P(None, "mn", "az", None), P())
    out_specs = P(None, "mn", "az", None)
    return jax.shard_map(
        on_device, mesh=mesh, in_specs=in_specs, out_specs=out_specs, check_vma=False
    )
```

profile of v0, /device:TPU:22, one launch (start us, length us, event | category | flops | bytes accessed | tf_op | source)
XLA Modules:
  0.0 249.8 jit_solution(7639540754251958149)
XLA Ops:
  0.0 2.2 fusion.81
  2.2 1.9 collective-permute-start
  4.2 12.6 %collective-permute-start.1 = (f32[41,8,2,128]{3,2,1,0:T(2,128)S(1)}, f32[41,8,2,128]{3,2,1,0:T(2,128)S(1)}, u32[]{:S(2)}, u32[]{:S(2)}) collective-permute-start(f32[41,8,2,128]{3,2,1,0:T(2,128)S(1)} %get-tuple-element.14), channel_id=1, source_target_pairs={{1,0},{2,1},{3,2},{4,3},{5,4},{6,5},{7,6},{8,7},{9,8},{10,9},{11,1... | collective-permute-start | bytes 1007624 | tf_op jit(solution)/shard_map/ppermute | solution.py:19
  16.8 3.1 %collective-permute-done = f32[41,8,2,128]{3,2,1,0:T(2,128)S(1)} collective-permute-done((f32[41,8,2,128]{3,2,1,0:T(2,128)S(1)}, f32[41,8,2,128]{3,2,1,0:T(2,128)S(1)}, u32[]{:S(2)}, u32[]{:S(2)}) %collective-permute-start) | collective-permute-done | bytes 335904 | tf_op jit(solution)/shard_map/ppermute | solution.py:18
  19.9 1.5 collective-permute-done.1
  22.7 3.4 %collective-permute-start.2 = (f32[41,2,12,128]{3,1,2,0:T(2,128)S(1)}, f32[41,2,12,128]{3,1,2,0:T(2,128)S(1)}, u32[]{:S(2)}, u32[]{:S(2)}) collective-permute-start(f32[41,2,12,128]{3,1,2,0:T(2,128)S(1)} %copy.55), channel_id=1, source_target_pairs={{8,0},{9,1},{10,2},{11,3},{12,4},{13,5},{14,6},{15,7},{0,8},{1,9},... | collective-permute-start | bytes 1511432 | tf_op jit(solution)/shard_map/ppermute | solution.py:27
  26.5 13.1 %collective-permute-start.3 = (f32[41,2,12,128]{3,1,2,0:T(2,128)S(1)}, f32[41,2,12,128]{3,1,2,0:T(2,128)S(1)}, u32[]{:S(2)}, u32[]{:S(2)}) collective-permute-start(f32[41,2,12,128]{3,1,2,0:T(2,128)S(1)} %copy.56), channel_id=1, source_target_pairs={{0,16},{16,32},{32,48},{48,64},{64,80},{80,96},{96,112},{112,128},... | collective-permute-start | bytes 1511432 | tf_op jit(solution)/shard_map/ppermute | solution.py:18
  39.6 2.1 collective-permute-start.4
  41.8 1.6 fusion.55
  43.5 27.0 %collective-permute-done.4 = f32[41,2,12,128]{3,1,2,0:T(2,128)S(1)} collective-permute-done((f32[41,2,12,128]{3,1,2,0:T(2,128)S(1)}, f32[41,2,12,128]{3,1,2,0:T(2,128)S(1)}, u32[]{:S(2)}, u32[]{:S(2)}) %collective-permute-start.4) | collective-permute-done | bytes 503840 | tf_op jit(solution)/shard_map/ppermute | solution.py:19
  70.6 43.5 %collective-permute-done.2 = f32[41,2,12,128]{3,1,2,0:T(2,128)S(1)} collective-permute-done((f32[41,2,12,128]{3,1,2,0:T(2,128)S(1)}, f32[41,2,12,128]{3,1,2,0:T(2,128)S(1)}, u32[]{:S(2)}, u32[]{:S(2)}) %collective-permute-start.2) | collective-permute-done | bytes 503840 | tf_op jit(solution)/shard_map/ppermute | solution.py:27
  115.4 3.5 %fusion.4 = f32[41,8,8,129]{3,2,1,0:T(8,128)S(1)} fusion(f32[41,8,8,128]{3,2,1,0:T(8,128)S(1)} %copy-done.1, f32[41,8,8,132]{3,2,1,0:T(8,128)S(1)} %pad_multiply_fusion.1, f32[8,8,129]{2,1,0:T(8,128)S(1)} %fusion.64), kind=kLoop, calls=%fused_computation.14 | loop fusion | flops 3046464 | bytes 5438464 | tf_op jit(solution)/shard_map/sub | solution.py:47
  119.9 1.6 fusion.40
  121.5 2.1 fusion.25
  126.2 1.9 collective-permute-start.5
  128.2 10.5 %collective-permute-start.6 = (f32[41,8,2,128]{3,2,1,0:T(2,128)S(1)}, f32[41,8,2,128]{3,2,1,0:T(2,128)S(1)}, u32[]{:S(2)}, u32[]{:S(2)}) collective-permute-start(f32[41,8,2,128]{3,2,1,0:T(2,128)S(1)} %get-tuple-element.11), channel_id=1, source_target_pairs={{1,0},{2,1},{3,2},{4,3},{5,4},{6,5},{7,6},{8,7},{9,8},{10,9},{11,1... | collective-permute-start | bytes 1007624 | tf_op jit(solution)/shard_map/ppermute | solution.py:19
  138.6 3.5 %fusion.11 = f32[41,8,8,129]{3,2,1,0:T(8,128)S(1)} fusion(f32[41,8,8,128]{3,2,1,0:T(8,128)S(1)} %fusion.51, f32[41,8,8,132]{3,2,1,0:T(8,128)S(1)} %pad_multiply_fusion, f32[8,8,129]{2,1,0:T(8,128)S(1)} %fusion.64), kind=kLoop, calls=%fused_computation.21 | loop fusion | flops 3046464 | bytes 5438464 | tf_op jit(solution)/shard_map/sub | solution.py:47
  142.2 1.7 fusion.57
  145.3 71.8 %collective-permute-start.7 = (f32[41,2,12,128]{3,1,2,0:T(2,128)S(1)}, f32[41,2,12,128]{3,1,2,0:T(2,128)S(1)}, u32[]{:S(2)}, u32[]{:S(2)}) collective-permute-start(f32[41,2,12,128]{3,1,2,0:T(2,128)S(1)} %copy.68), channel_id=1, source_target_pairs={{8,0},{9,1},{10,2},{11,3},{12,4},{13,5},{14,6},{15,7},{0,8},{1,9},... | collective-permute-start | bytes 1511432 | tf_op jit(solution)/shard_map/ppermute | solution.py:27
  217.3 1.9 collective-permute-start.8
  219.3 3.9 %collective-permute-start.9 = (f32[41,2,12,128]{3,1,2,0:T(2,128)S(1)}, f32[41,2,12,128]{3,1,2,0:T(2,128)S(1)}, u32[]{:S(2)}, u32[]{:S(2)}) collective-permute-start(f32[41,2,12,128]{3,1,2,0:T(2,128)S(1)} %copy.72), channel_id=1, source_target_pairs={{16,0},{32,16},{48,32},{64,48},{80,64},{96,80},{112,96},{128,112},... | collective-permute-start | bytes 1511432 | tf_op jit(solution)/shard_map/ppermute | solution.py:19
  223.2 2.2 fusion.17
  225.4 19.4 %collective-permute-done.9 = f32[41,2,12,128]{3,1,2,0:T(2,128)S(1)} collective-permute-done((f32[41,2,12,128]{3,1,2,0:T(2,128)S(1)}, f32[41,2,12,128]{3,1,2,0:T(2,128)S(1)}, u32[]{:S(2)}, u32[]{:S(2)}) %collective-permute-start.9) | collective-permute-done | bytes 503840 | tf_op jit(solution)/shard_map/ppermute | solution.py:19
  245.4 1.6 fusion.33
  (57 shorter events, 11.7 us)
Async XLA Ops:
  0.0 41.8 %copy-start = (f32[30,30]{1,0:T(8,128)S(1)}, f32[30,30]{1,0:T(8,128)}, u32[]{:S(2)}) copy-start(f32[30,30]{1,0:T(8,128)} %param.3) | copy-start | bytes 10804
  0.0 16.8 %copy-start.1 = (f32[41,8,8,128]{3,2,1,0:T(8,128)S(1)}, f32[41,8,8,128]{3,2,1,0:T(8,128)}, u32[]{:S(2)}) copy-start(f32[41,8,8,128]{3,2,1,0:T(8,128)} %param.2) | copy-start | bytes 4030468
  2.2 17.6 %collective-permute-start = (f32[41,8,2,128]{3,2,1,0:T(2,128)S(1)}, f32[41,8,2,128]{3,2,1,0:T(2,128)S(1)}, u32[]{:S(2)}, u32[]{:S(2)}) collective-permute-start(f32[41,8,2,128]{3,2,1,0:T(2,128)S(1)} %get-tuple-element.13), channel_id=1, source_target_pairs={{0,1},{1,2},{2,3},{3,4},{4,5},{5,6},{6,7},{7,8},{8,9},{9,10},{10,1... | collective-permute-start | bytes 1007624 | tf_op jit(solution)/shard_map/ppermute | solution.py:18
  4.2 17.3 %collective-permute-start.1 = (f32[41,8,2,128]{3,2,1,0:T(2,128)S(1)}, f32[41,8,2,128]{3,2,1,0:T(2,128)S(1)}, u32[]{:S(2)}, u32[]{:S(2)}) collective-permute-start(f32[41,8,2,128]{3,2,1,0:T(2,128)S(1)} %get-tuple-element.14), channel_id=1, source_target_pairs={{1,0},{2,1},{3,2},{4,3},{5,4},{6,5},{7,6},{8,7},{9,8},{10,9},{11,1... | collective-permute-start | bytes 1007624 | tf_op jit(solution)/shard_map/ppermute | solution.py:19
  22.7 19.1 %slice-start = ((f32[41,8,8,128]{3,2,1,0:T(8,128)}), f32[30,8,8,128]{3,2,1,0:T(8,128)S(1)}, s32[]{:S(2)}) async-start(f32[41,8,8,128]{3,2,1,0:T(8,128)} %param.2), calls=%async_computation | async-start | bytes 1966080 | tf_op jit(solution)/shard_map/slice | solution.py:70
  22.7 91.3 %collective-permute-start.2 = (f32[41,2,12,128]{3,1,2,0:T(2,128)S(1)}, f32[41,2,12,128]{3,1,2,0:T(2,128)S(1)}, u32[]{:S(2)}, u32[]{:S(2)}) collective-permute-start(f32[41,2,12,128]{3,1,2,0:T(2,128)S(1)} %copy.55), channel_id=1, source_target_pairs={{8,0},{9,1},{10,2},{11,3},{12,4},{13,5},{14,6},{15,7},{0,8},{1,9},... | collective-permute-start | bytes 1511432 | tf_op jit(solution)/shard_map/ppermute | solution.py:27
  26.5 87.6 %collective-permute-start.3 = (f32[41,2,12,128]{3,1,2,0:T(2,128)S(1)}, f32[41,2,12,128]{3,1,2,0:T(2,128)S(1)}, u32[]{:S(2)}, u32[]{:S(2)}) collective-permute-start(f32[41,2,12,128]{3,1,2,0:T(2,128)S(1)} %copy.56), channel_id=1, source_target_pairs={{0,16},{16,32},{32,48},{48,64},{64,80},{80,96},{96,112},{112,128},... | collective-permute-start | bytes 1511432 | tf_op jit(solution)/shard_map/ppermute | solution.py:18
  39.6 30.9 %collective-permute-start.4 = (f32[41,2,12,128]{3,1,2,0:T(2,128)S(1)}, f32[41,2,12,128]{3,1,2,0:T(2,128)S(1)}, u32[]{:S(2)}, u32[]{:S(2)}) collective-permute-start(f32[41,2,12,128]{3,1,2,0:T(2,128)S(1)} %copy.59), channel_id=1, source_target_pairs={{16,0},{32,16},{48,32},{64,48},{80,64},{96,80},{112,96},{128,112},... | collective-permute-start | bytes 1511432 | tf_op jit(solution)/shard_map/ppermute | solution.py:19
  126.2 17.7 %collective-permute-start.5 = (f32[41,8,2,128]{3,2,1,0:T(2,128)S(1)}, f32[41,8,2,128]{3,2,1,0:T(2,128)S(1)}, u32[]{:S(2)}, u32[]{:S(2)}) collective-permute-start(f32[41,8,2,128]{3,2,1,0:T(2,128)S(1)} %get-tuple-element.12), channel_id=1, source_target_pairs={{0,1},{1,2},{2,3},{3,4},{4,5},{5,6},{6,7},{7,8},{8,9},{9,10},{10,1... | collective-permute-start | bytes 1007624 | tf_op jit(solution)/shard_map/ppermute | solution.py:18
  128.2 15.7 %collective-permute-start.6 = (f32[41,8,2,128]{3,2,1,0:T(2,128)S(1)}, f32[41,8,2,128]{3,2,1,0:T(2,128)S(1)}, u32[]{:S(2)}, u32[]{:S(2)}) collective-permute-start(f32[41,8,2,128]{3,2,1,0:T(2,128)S(1)} %get-tuple-element.11), channel_id=1, source_target_pairs={{1,0},{2,1},{3,2},{4,3},{5,4},{6,5},{7,6},{8,7},{9,8},{10,9},{11,1... | collective-permute-start | bytes 1007624 | tf_op jit(solution)/shard_map/ppermute | solution.py:19
  145.3 99.6 %collective-permute-start.7 = (f32[41,2,12,128]{3,1,2,0:T(2,128)S(1)}, f32[41,2,12,128]{3,1,2,0:T(2,128)S(1)}, u32[]{:S(2)}, u32[]{:S(2)}) collective-permute-start(f32[41,2,12,128]{3,1,2,0:T(2,128)S(1)} %copy.68), channel_id=1, source_target_pairs={{8,0},{9,1},{10,2},{11,3},{12,4},{13,5},{14,6},{15,7},{0,8},{1,9},... | collective-permute-start | bytes 1511432 | tf_op jit(solution)/shard_map/ppermute | solution.py:27
  217.3 27.6 %collective-permute-start.8 = (f32[41,2,12,128]{3,1,2,0:T(2,128)S(1)}, f32[41,2,12,128]{3,1,2,0:T(2,128)S(1)}, u32[]{:S(2)}, u32[]{:S(2)}) collective-permute-start(f32[41,2,12,128]{3,1,2,0:T(2,128)S(1)} %copy.69), channel_id=1, source_target_pairs={{0,16},{16,32},{32,48},{48,64},{64,80},{80,96},{96,112},{112,128},... | collective-permute-start | bytes 1511432 | tf_op jit(solution)/shard_map/ppermute | solution.py:18
  219.3 25.5 %collective-permute-start.9 = (f32[41,2,12,128]{3,1,2,0:T(2,128)S(1)}, f32[41,2,12,128]{3,1,2,0:T(2,128)S(1)}, u32[]{:S(2)}, u32[]{:S(2)}) collective-permute-start(f32[41,2,12,128]{3,1,2,0:T(2,128)S(1)} %copy.72), channel_id=1, source_target_pairs={{16,0},{32,16},{48,32},{64,48},{80,64},{96,80},{112,96},{128,112},... | collective-permute-start | bytes 1511432 | tf_op jit(solution)/shard_map/ppermute | solution.py:19
where the time goes:
time: 250 us
  starting transfers between devices  123 us (49%)
  waiting for transfers between devices  94.5 us (38%)
  other arithmetic  23.5 us (9%)
  local copies, waits for them, and re-layouts  4.9 us (2%)
  matrix products  3.26 us (1%)
    ppermute x2, starting transfers between devices, from_behind(): return lax.ppermute(block, axis, route)  75.2 us
    ppermute x4, waiting for transfers between devices, with_halo(): after = lax.ppermute(first, axis, down)  47.9 us
    ppermute x2, waiting for transfers between devices, from_behind(): return lax.ppermute(block, axis, route)  43.5 us
    ppermute x4, starting transfers between devices, with_halo(): after = lax.ppermute(first, axis, down)  29.1 us
    ppermute x4, starting transfers between devices, with_halo(): before = lax.ppermute(last, axis, up)  18.9 us
    sub x6, other arithmetic, face_div(): 0.5 * (window(carried, 1) + window(carried, 2))  14.5 us
  transfers between devices with their start and end apart: 10, of which 5 were waited for; matrix products, arithmetic and copies ran while one was open for 4% of the time, Pallas kernels for 0%

commit v1 on v0

v1 whole, which is shorter than its diff:
```python
import functools

import jax
import jax.numpy as jnp
from jax import lax
from jax.experimental import pallas as pl
from jax.experimental.pallas import tpu as pltpu
from jax.sharding import PartitionSpec as P

MESH = pl.DeviceIdType.MESH
DISSIPATION = 0.05
SOUND_SPEED = 1.0
TIME_STEP = 0.3
NQ, NLEV, FIRST_LEVEL, ELECTRON = 41, 30, 11, 10
ROWS, LANES = 8, 128
COLUMNS = 4
BOUNDS = (0, 11, 21, 31, 41)


def parts_of(a, b):
    cuts = [a + ((b - a) * p + COLUMNS - 1) // COLUMNS for p in range(COLUMNS + 1)]
    return [(cuts[p], cuts[p + 1]) for p in range(COLUMNS)]


CHUNKS = [(a, b, parts_of(a, b)) for a, b in zip(BOUNDS[:-1], BOUNDS[1:])]
NC = len(CHUNKS)


def as_int(flag):
    return flag.astype(jnp.int32)


def kernel(flow, rates, out, q, s1, new, coef, halo, hk, rf, rb,
           in_sem, out_sem, s_far, s_near, s_az, s_rel, r_halo, r_rel, r_az):
    mn, az = lax.axis_index("mn"), lax.axis_index("az")
    n_mn, n_az = lax.axis_size("mn"), lax.axis_size("az")
    groups = n_mn // COLUMNS
    x, m = lax.rem(mn, COLUMNS), lax.div(mn, COLUMNS)
    opp = lax.rem(az + n_az // 2, n_az)
    az_up, az_dn = lax.rem(az + 1, n_az), lax.rem(az + n_az - 1, n_az)
    pole = mn == 0
    first, last = x == 0, x == COLUMNS - 1
    up_far = last & (m < groups - 1)
    f_to = (4 * m + 4, az)
    b_to = (jnp.where(pole | (m == 0), 0, 4 * m - 1), jnp.where(m == 0, opp, az))
    b_side = jnp.where(m == 0, 0, 1)

    bar = pltpu.get_barrier_semaphore()

    def tell(cond, device):
        @pl.when(cond)
        def _():
            pl.semaphore_signal(bar, 1, device_id=device, device_id_type=MESH)

    far_az = jnp.where(pole, opp, az)
    tell(first, (jnp.where(pole, 0, mn - 1), far_az))
    for p in range(3):
        tell(first, (jnp.where(pole, p + 1, mn - 4 + p), far_az))
        tell(up_far, (mn + 2 + p, az))
    tell(up_far, (mn + 1, az))
    tell(jnp.logical_not(last) & (m < groups - 1), (4 * m + 3, az))
    tell(jnp.logical_not(first), (4 * m, az))
    tell(jnp.logical_not(first), (mn - 1, az))
    tell(jnp.logical_not(last), (mn + 1, az))
    for other in (az_up, az_dn):
        pl.semaphore_signal(bar, 1, device_id=(mn, other), device_id_type=MESH)
    targets = 2 + 4 * as_int(first) + 4 * as_int(up_far) + 2 * as_int(jnp.logical_not(first))
    targets += as_int(jnp.logical_not(last)) + as_int(jnp.logical_not(last) & (m < groups - 1))

    load = pltpu.make_async_copy(flow, q, in_sem)
    load.start()

    @pl.when(mn == n_mn - 1)
    def _():
        for e in range(2):
            halo[e, 1] = jnp.zeros((NQ, 2, ROWS, LANES), jnp.float32)

    load.wait()

    def source(field, acc):
        def pair(t, _):
            a = 2 * t
            sums = [[None] * ROWS, [None] * ROWS]
            for b in range(NLEV):
                r0, r1 = rates[a, b], rates[a + 1, b]
                for i in range(ROWS):
                    v = field[FIRST_LEVEL + b, i]
                    for s, r in ((0, r0), (1, r1)):
                        term = v * r
                        sums[s][i] = term if b == 0 else sums[s][i] + term
            for i in range(ROWS):
                scale = TIME_STEP * field[ELECTRON, i]
                for s in range(2):
                    acc[FIRST_LEVEL + a + s, i] = scale * sums[s][i]
            return 0
        lax.fori_loop(0, NLEV // 2, pair, 0)

    source(q, s1)
    pl.semaphore_wait(bar, targets)

    started = []

    def copy(src, dst, s, r, device):
        return pltpu.make_async_remote_copy(src, dst, s, r, device_id=device, device_id_type=MESH)

    def start(cond, c):
        if cond is None:
            c.start()
        else:
            pl.when(cond)(lambda: c.start())
        started.append((cond, c))

    def send_far(e, c, field):
        _, _, parts = CHUNKS[c]
        for p in range(4):
            a, b = parts[p]
            if p == 3:
                start(up_far, copy(field.at[a:b, 6:8], halo.at[e, 0, a:b], s_far.at[e, 0, c, p], r_halo.at[e, 0, c, p], f_to))
            else:
                start(up_far, copy(field.at[a:b, 6:8], rf.at[e, a:b], s_far.at[e, 0, c, p], r_rel.at[e, 0, c], (4 * m + p, az)))
            p = 3 - p
            a, b = parts[p]
            if p == 0:
                start(first, copy(field.at[a:b, 0:2], halo.at[e, b_side, a:b], s_far.at[e, 1, c, p], r_halo.at[e, b_side, c, p], b_to))
            else:
                start(first, copy(field.at[a:b, 0:2], rb.at[e, a:b], s_far.at[e, 1, c, p], r_rel.at[e, 1, c], (4 * m + p, az)))

    def send_az(e, c, field):
        a, b, _ = CHUNKS[c]
        start(None, copy(field.at[a:b, :, 0:2], hk.at[e, a:b, :, 0:2], s_az.at[e, 0, c], r_az.at[e, 0, c], (mn, az_dn)))
        start(None, copy(field.at[a:b, :, 6:8], hk.at[e, a:b, :, 6:8], s_az.at[e, 1, c], r_az.at[e, 1, c], (mn, az_up)))

    def send_near(e, c, field):
        a, b, _ = CHUNKS[c]
        start(jnp.logical_not(last), copy(field.at[a:b, 6:8], halo.at[e, 0, a:b], s_near.at[e, 0, c], r_halo.at[e, 0, c, 0], (mn + 1, az)))
        start(jnp.logical_not(first), copy(field.at[a:b, 0:2], halo.at[e, 1, a:b], s_near.at[e, 1, c], r_halo.at[e, 1, c, 0], (mn - 1, az)))

    def await_copy(cond, dst, r):
        c = copy(dst, dst, in_sem, r, f_to)
        if cond is None:
            c.wait_recv()
        else:
            pl.when(cond)(lambda: c.wait_recv())

    def relay(e, c):
        _, _, parts = CHUNKS[c]
        for p in range(4):
            a, b = parts[p]
            if p != 3:
                cond = (x == p) & (m < groups - 1)
                await_copy(cond, rf.at[e, a:b], r_rel.at[e, 0, c])
                start(cond, copy(rf.at[e, a:b], halo.at[e, 0, a:b], s_rel.at[e, 0, c], r_halo.at[e, 0, c, p], f_to))
            if p != 0:
                cond = x == p
                await_copy(cond, rb.at[e, a:b], r_rel.at[e, 1, c])
                start(cond, copy(rb.at[e, a:b], halo.at[e, b_side, a:b], s_rel.at[e, 1, c], r_halo.at[e, b_side, c, p], b_to))

    def await_margins(e, c):
        a, b, parts = CHUNKS[c]
        await_copy(None, hk.at[e, a:b, :, 0:2], r_az.at[e, 0, c])
        await_copy(None, hk.at[e, a:b, :, 6:8], r_az.at[e, 1, c])
        await_copy(jnp.logical_not(first), halo.at[e, 0, a:b], r_halo.at[e, 0, c, 0])
        await_copy(jnp.logical_not(last), halo.at[e, 1, a:b], r_halo.at[e, 1, c, 0])
        for p in range(4):
            pa, pb = parts[p]
            await_copy(first, halo.at[e, 0, pa:pb], r_halo.at[e, 0, c, p])
            await_copy(up_far, halo.at[e, 1, pa:pb], r_halo.at[e, 1, c, p])
        if c == 0:
            @pl.when(pole)
            def _():
                for n in (5, 7):
                    halo[e, 0, n] = -halo[e, 0, n]

    below = (jnp.where(pole, 0, 1), jnp.where(pole, 1, 0))

    def row(e, field, n, i):
        if i < 0:
            return halo[e, 0, n, below[-i - 1]]
        if i >= ROWS:
            return halo[e, 1, n, i - ROWS]
        return field[n, i]

    k_at = lax.broadcasted_iota(jnp.int32, (ROWS, LANES), 0)
    j_at = lax.broadcasted_iota(jnp.int32, (ROWS, LANES), 1)

    def along_k(v, h):
        return [
            pltpu.roll(jnp.where(k_at < 1, h, v), 7, 0),
            pltpu.roll(jnp.where(k_at < 2, h, v), 6, 0),
            pltpu.roll(jnp.where(k_at >= 7, h, v), 1, 0),
            pltpu.roll(jnp.where(k_at >= 6, h, v), 2, 0),
        ]

    def speed(u, v):
        return DISSIPATION * (0.5 * (jnp.abs(u) + jnp.abs(v)) + SOUND_SPEED)

    def taps(u_m, u, u_p):
        s_m, s_p = speed(u_m, u), speed(u, u_p)
        return (
            TIME_STEP * (-0.5 * u_p - 3.0 * s_p - s_m),
            TIME_STEP * s_p,
            TIME_STEP * (0.5 * u_m - s_p - 3.0 * s_m),
            TIME_STEP * s_m,
            (3.0 * TIME_STEP) * (s_p + s_m),
        )

    def coefficients():
        def density(read):
            return 1.0 / jnp.maximum(read(0) + read(1) + read(2) + read(3) + read(4), 1.0)

        def u_i(i):
            return row(0, q, 5, i) * density(lambda n: row(0, q, n, i))

        u_m, u = u_i(-1), u_i(0)
        for i in range(ROWS):
            u_p = u_i(i + 1)
            inverse = density(lambda n: q[n, i])
            ti = taps(u_m, u, u_p)
            u_m, u = u, u_p
            uk = q[7, i] * inverse
            hk_u = hk[0, 7, i] * density(lambda n: hk[0, n, i])
            shifted = along_k(uk, hk_u)
            tk = taps(shifted[2], uk, shifted[0])
            uj = q[6, i] * inverse
            uj_p = jnp.where(j_at < LANES - 1, pltpu.roll(uj, LANES - 1, 1), 0.0)
            uj_m = jnp.where(j_at > 0, pltpu.roll(uj, 1, 1), 0.0)
            tj = taps(uj_m, uj, uj_p)
            for t in range(4):
                coef[t, i] = ti[t]
                coef[4 + t, i] = tk[t]
            coef[8, i] = jnp.where(j_at < LANES - 1, tj[0], 0.0)
            coef[9, i] = jnp.where(j_at < LANES - 2, tj[1], 0.0)
            coef[10, i] = jnp.where(j_at > 0, tj[2], 0.0)
            coef[11, i] = jnp.where(j_at > 1, tj[3], 0.0)
            coef[12, i] = 1.0 + ti[4] + tk[4] + tj[4]

    def section(e, field, acc, a, b, chemistry, final):
        for i in range(ROWS):
            cs = [coef[t, i] for t in range(13)]

            def one(n, _):
                v = field[n, i]
                r = cs[12] * v
                for t, d in enumerate((1, 2, -1, -2)):
                    r = r + cs[t] * row(e, field, n, i + d)
                ks = along_k(v, hk[e, n, i])
                for t in range(4):
                    r = r + cs[4 + t] * ks[t]
                for t, d in enumerate((1, 2, -1, -2)):
                    r = r + cs[8 + t] * pltpu.roll(v, (LANES - d) % LANES, 1)
                if chemistry:
                    r = r + acc[n, i]
                acc[n, i] = 0.5 * (q[n, i] + r) if final else r
                return 0

            lax.fori_loop(a, b, one, 0)

    for c in range(NC):
        send_far(0, c, q)
    for c in range(NC):
        send_az(0, c, q)
    for c in range(NC):
        send_near(0, c, q)
    for c in range(NC):
        relay(0, c)
    for c in range(NC):
        a, b, _ = CHUNKS[c]
        await_margins(0, c)
        if c == 0:
            coefficients()
        section(0, q, s1, a, b, c > 0, False)
        send_far(1, c, s1)
        send_az(1, c, s1)
        send_near(1, c, s1)
        relay(1, c)
    source(s1, new)
    stores = []
    for c in range(NC):
        a, b, _ = CHUNKS[c]
        await_margins(1, c)
        section(1, s1, new, a, b, c > 0, True)
        store = pltpu.make_async_copy(new.at[a:b], out.at[a:b], out_sem.at[c])
        store.start()
        stores.append(store)
    for cond, c in started:
        if cond is None:
            c.wait_send()
        else:
            pl.when(cond)(lambda c=c: c.wait_send())
    for store in stores:
        store.wait()


def on_device(flow_state, level_rates):
    def vmem(*shape):
        return pltpu.VMEM(shape, jnp.float32)

    def sems(*shape):
        return pltpu.SemaphoreType.DMA(shape)

    block = (NQ, ROWS, ROWS, LANES)
    margin = (NQ, 2, ROWS, LANES)
    return pl.pallas_call(
        kernel,
        out_shape=jax.ShapeDtypeStruct(block, jnp.float32),
        in_specs=[pl.BlockSpec(memory_space=pl.ANY), pl.BlockSpec(memory_space=pltpu.SMEM)],
        out_specs=pl.BlockSpec(memory_space=pl.ANY),
        scratch_shapes=[
            vmem(*block), vmem(*block), vmem(*block), vmem(13, ROWS, ROWS, LANES),
            vmem(2, 2, *margin), vmem(2, *block), vmem(2, *margin), vmem(2, *margin),
            pltpu.SemaphoreType.DMA, sems(NC), sems(2, 2, NC, 4), sems(2, 2, NC), sems(2, 2, NC), sems(2, 2, NC),
            sems(2, 2, NC, 4), sems(2, 2, NC), sems(2, 2, NC),
        ],
        compiler_params=pltpu.CompilerParams(
            collective_id=0, has_side_effects=True, vmem_limit_bytes=40 * 1024 * 1024
        ),
    )(flow_state, level_rates)


def solution(mesh):
    in_specs = (P(None, "mn", "az", None), P())
    out_specs = P(None, "mn", "az", None)
    return jax.shard_map(
        on_device, mesh=mesh, in_specs=in_specs, out_specs=out_specs, check_vma=False
    )
```

time: 250 us -> 124 us (0.50)
  the two profiles are of different devices: /device:TPU:22 before, /device:TPU:2 now
where the time goes in v1:
time: 124 us
  Pallas kernels  121 us (98%)
  local copies, waits for them, and re-layouts  3.11 us (3%)
    pallas_call x1, Pallas kernels, on_device(): pl.pallas_call(kernel, out_shape=jax.ShapeDtypeStruct(block, jnp.float32)...  121 us
    unnamed x5, local copies, waits for them, and re-layouts  3.11 us

profile of v1, /device:TPU:2, one launch (start us, length us, event | category | flops | bytes accessed | tf_op | source)
XLA Modules:
  0.0 124.1 jit_solution(15857501440051226346)
XLA Ops:
  0.0 0.0 copy-start
  0.0 1.3 %copy-done = f32[41,8,8,128]{3,2,1,0:T(8,128)S(1)} copy-done((f32[41,8,8,128]{3,2,1,0:T(8,128)S(1)}, f32[41,8,8,128]{3,2,1,0:T(8,128)}, u32[]{:S(2)}) %copy-start) | copy-done | bytes 1343512
  1.3 0.0 copy-start.1
  1.3 0.7 copy-done.1
  2.0 121.0 %shard_map.28 = f32[41,8,8,128]{3,2,1,0:T(8,128)S(1)} custom-call(f32[41,8,8,128]{3,2,1,0:T(8,128)S(1)} %copy-done, f32[30,30]{1,0:T(8,128)S(1)} %copy-done.1), custom_call_target="tpu_custom_call" | custom-call | tf_op jit(solution)/shard_map/pallas_call | solution.py:303
  123.1 1.1 copy.4
Async XLA Ops:
  0.0 1.3 %copy-start = (f32[41,8,8,128]{3,2,1,0:T(8,128)S(1)}, f32[41,8,8,128]{3,2,1,0:T(8,128)}, u32[]{:S(2)}) copy-start(f32[41,8,8,128]{3,2,1,0:T(8,128)} %flow.1) | copy-start | bytes 4030468
  1.3 0.7 copy-start.1

commit v2 on v1

--- a/solution.py
+++ b/solution.py
@@ -15,6 +15,7 @@
 ROWS, LANES = 8, 128
 COLUMNS = 4
 BOUNDS = (0, 11, 21, 31, 41)
+UNROLL = 10
 
 
 def parts_of(a, b):
@@ -238,22 +239,28 @@
         for i in range(ROWS):
             cs = [coef[t, i] for t in range(13)]
 
-            def one(n, _):
+            def one(n):
                 v = field[n, i]
-                r = cs[12] * v
-                for t, d in enumerate((1, 2, -1, -2)):
-                    r = r + cs[t] * row(e, field, n, i + d)
                 ks = along_k(v, hk[e, n, i])
-                for t in range(4):
-                    r = r + cs[4 + t] * ks[t]
-                for t, d in enumerate((1, 2, -1, -2)):
-                    r = r + cs[8 + t] * pltpu.roll(v, (LANES - d) % LANES, 1)
+                js = [pltpu.roll(v, (LANES - d) % LANES, 1) for d in (1, 2, -1, -2)]
+                rows = [row(e, field, n, i + d) for d in (1, 2, -1, -2)]
+                sums = [cs[12] * v]
+                for base, values in ((0, rows), (4, ks), (8, js)):
+                    t = [cs[base + d] * values[d] for d in range(4)]
+                    sums.append((t[0] + t[1]) + (t[2] + t[3]))
+                r = (sums[0] + sums[1]) + (sums[2] + sums[3])
                 if chemistry:
                     r = r + acc[n, i]
                 acc[n, i] = 0.5 * (q[n, i] + r) if final else r
+
+            def several(g, _):
+                for s in range(UNROLL):
+                    one(a + g * UNROLL + s)
                 return 0
 
-            lax.fori_loop(a, b, one, 0)
+            lax.fori_loop(0, (b - a) // UNROLL, several, 0)
+            for n in range(a + (b - a) // UNROLL * UNROLL, b):
+                one(n)
 
     for c in range(NC):
         send_far(0, c, q)

time: 124 us -> 94.7 us (0.76)
  Pallas kernels: 121 us -> 91.4 us
    pallas_call x1, Pallas kernels: 121 us -> 91.4 us  [on_device(): pl.pallas_call(kernel, out_shape=jax.ShapeDtypeStruct(block, jnp.float32)...]
where the time goes in v2:
time: 94.7 us; the launch traced here: 94.5 us
  Pallas kernels  91.4 us (97%)
  local copies, waits for them, and re-layouts  3.11 us (3%)
    pallas_call x1, Pallas kernels, on_device(): pl.pallas_call(kernel, out_shape=jax.ShapeDtypeStruct(block, jnp.float32)...  91.4 us
    unnamed x5, local copies, waits for them, and re-layouts  3.11 us

profile of v2, /device:TPU:2, one launch (start us, length us, event | category | flops | bytes accessed | tf_op | source)
XLA Modules:
  0.0 94.5 jit_solution(17588338436140280393)
XLA Ops:
  0.0 0.0 copy-start
  0.0 1.3 %copy-done = f32[41,8,8,128]{3,2,1,0:T(8,128)S(1)} copy-done((f32[41,8,8,128]{3,2,1,0:T(8,128)S(1)}, f32[41,8,8,128]{3,2,1,0:T(8,128)}, u32[]{:S(2)}) %copy-start) | copy-done | bytes 1343512
  1.3 0.0 copy-start.1
  1.3 0.7 copy-done.1
  2.0 91.4 %shard_map.28 = f32[41,8,8,128]{3,2,1,0:T(8,128)S(1)} custom-call(f32[41,8,8,128]{3,2,1,0:T(8,128)S(1)} %copy-done, f32[30,30]{1,0:T(8,128)S(1)} %copy-done.1), custom_call_target="tpu_custom_call" | custom-call | tf_op jit(solution)/shard_map/pallas_call | solution.py:310
  93.5 1.1 %copy.4 = f32[41,8,8,128]{3,2,1,0:T(8,128)} copy(f32[41,8,8,128]{3,2,1,0:T(8,128)S(1)} %shard_map.28) | data formatting | bytes 2686976
Async XLA Ops:
  0.0 1.3 %copy-start = (f32[41,8,8,128]{3,2,1,0:T(8,128)S(1)}, f32[41,8,8,128]{3,2,1,0:T(8,128)}, u32[]{:S(2)}) copy-start(f32[41,8,8,128]{3,2,1,0:T(8,128)} %flow.1) | copy-start | bytes 4030468
  1.3 0.7 copy-start.1

commit v3 on v2

--- a/solution.py
+++ b/solution.py
@@ -16,6 +16,7 @@
 COLUMNS = 4
 BOUNDS = (0, 11, 21, 31, 41)
 UNROLL = 10
+POLE_GROUP, POLE_CHUNKS = 6, (1, 3)
 
 
 def parts_of(a, b):
@@ -31,8 +32,8 @@
     return flag.astype(jnp.int32)
 
 
-def kernel(flow, rates, out, q, s1, new, coef, halo, hk, rf, rb,
-           in_sem, out_sem, s_far, s_near, s_az, s_rel, r_halo, r_rel, r_az):
+def kernel(flow, rates, out, q, s1, new, coef, halo, hk, rf, rb, rp,
+           in_sem, out_sem, s_far, s_near, s_az, s_rel, r_halo, r_rel, r_az, far_sem, pole_sem, wrap_sem):
     mn, az = lax.axis_index("mn"), lax.axis_index("az")
     n_mn, n_az = lax.axis_size("mn"), lax.axis_size("az")
     groups = n_mn // COLUMNS
@@ -46,27 +47,37 @@
     b_to = (jnp.where(pole | (m == 0), 0, 4 * m - 1), jnp.where(m == 0, opp, az))
     b_side = jnp.where(m == 0, 0, 1)
 
+    even, odd = lax.rem(m, 2) == 0, lax.rem(m, 2) == 1
+    g0, g6 = m == 0, m == POLE_GROUP
+    low_z, high_z = az < n_az // 2, az >= n_az // 2
+    above = m < groups - 1
     bar = pltpu.get_barrier_semaphore()
 
-    def tell(cond, device):
-        @pl.when(cond)
-        def _():
-            pl.semaphore_signal(bar, 1, device_id=device, device_id_type=MESH)
-
-    far_az = jnp.where(pole, opp, az)
-    tell(first, (jnp.where(pole, 0, mn - 1), far_az))
+    def tell(cond, device, sem=bar):
+        def signal():
+            pl.semaphore_signal(sem, 1, device_id=device, device_id_type=MESH)
+        if cond is None:
+            signal()
+        else:
+            pl.when(cond)(signal)
+
+    for d in range(1, 4):
+        tell(None, (4 * m + lax.rem(x + d, 4), az))
+    tell(None, (mn, az_dn))
+    tell(az < n_az - 1, (mn, az_up))
+    tell(even, (4 * m + 4, az))
+    tell(even & (m > 0), (4 * m - 1, az))
     for p in range(3):
-        tell(first, (jnp.where(pole, p + 1, mn - 4 + p), far_az))
-        tell(up_far, (mn + 2 + p, az))
-    tell(up_far, (mn + 1, az))
-    tell(jnp.logical_not(last) & (m < groups - 1), (4 * m + 3, az))
-    tell(jnp.logical_not(first), (4 * m, az))
-    tell(jnp.logical_not(first), (mn - 1, az))
-    tell(jnp.logical_not(last), (mn + 1, az))
-    for other in (az_up, az_dn):
-        pl.semaphore_signal(bar, 1, device_id=(mn, other), device_id_type=MESH)
-    targets = 2 + 4 * as_int(first) + 4 * as_int(up_far) + 2 * as_int(jnp.logical_not(first))
-    targets += as_int(jnp.logical_not(last)) + as_int(jnp.logical_not(last) & (m < groups - 1))
+        tell(even & first & (m > 0), (4 * m - 4 + p, az))
+        tell(even & last, (4 * m + 5 + p, az))
+        tell(pole & low_z, (p + 1, opp))
+    tell((g0 | g6) & low_z, (0, opp))
+    for p in range(4):
+        tell(pole & low_z, (4 * POLE_GROUP + p, opp))
+    tell(g6, (0, az))
+    targets = 5 - as_int(az == 0) + 4 * as_int(pole) + as_int(odd) + 3 * as_int(odd & first)
+    targets += as_int(odd & above) + 3 * as_int(odd & above & last)
+    targets += 8 * as_int(pole & high_z) + as_int(((g0 & (x > 0)) | g6) & high_z)
 
     load = pltpu.make_async_copy(flow, q, in_sem)
     load.start()
@@ -96,8 +107,13 @@
             return 0
         lax.fori_loop(0, NLEV // 2, pair, 0)
 
-    source(q, s1)
     pl.semaphore_wait(bar, targets)
+    for p in range(4):
+        tell(odd & first, (4 * m - 4 + p, az), far_sem)
+        tell(odd & last & above, (4 * m + 4 + p, az), far_sem)
+        tell(pole & high_z, (p, opp), pole_sem)
+        tell(pole & high_z, (4 * POLE_GROUP + p, opp), pole_sem)
+    tell(az == n_az - 1, (mn, az_up), wrap_sem)
 
     started = []
 
@@ -111,25 +127,37 @@
             pl.when(cond)(lambda: c.start())
         started.append((cond, c))
 
-    def send_far(e, c, field):
+    def send_to_relays(e, c, field):
         _, _, parts = CHUNKS[c]
-        for p in range(4):
-            a, b = parts[p]
-            if p == 3:
-                start(up_far, copy(field.at[a:b, 6:8], halo.at[e, 0, a:b], s_far.at[e, 0, c, p], r_halo.at[e, 0, c, p], f_to))
-            else:
+        for p, (a, b) in enumerate(parts):
+            if p != 3:
                 start(up_far, copy(field.at[a:b, 6:8], rf.at[e, a:b], s_far.at[e, 0, c, p], r_rel.at[e, 0, c], (4 * m + p, az)))
-            p = 3 - p
-            a, b = parts[p]
-            if p == 0:
-                start(first, copy(field.at[a:b, 0:2], halo.at[e, b_side, a:b], s_far.at[e, 1, c, p], r_halo.at[e, b_side, c, p], b_to))
-            else:
-                start(first, copy(field.at[a:b, 0:2], rb.at[e, a:b], s_far.at[e, 1, c, p], r_rel.at[e, 1, c], (4 * m + p, az)))
+            if p != 0:
+                cond = first & (m > 0) if c in POLE_CHUNKS else first
+                start(cond, copy(field.at[a:b, 0:2], rb.at[e, a:b], s_far.at[e, 1, c, p], r_rel.at[e, 1, c], (4 * m + p, az)))
+            if c in POLE_CHUNKS:
+                start(pole, copy(field.at[a:b, 0:2], rp.at[e, a:b], s_far.at[e, 2, c, p], r_rel.at[e, 2, c], (4 * POLE_GROUP + p, az)))
+
+    def send_direct(e, c, field, across):
+        _, _, parts = CHUNKS[c]
+        a, b = parts[3]
+        if not across:
+            start(up_far, copy(field.at[a:b, 6:8], halo.at[e, 0, a:b], s_far.at[e, 0, c, 3], r_halo.at[e, 0, c, 3], f_to))
+        a, b = parts[0]
+        if not across or c not in POLE_CHUNKS:
+            cond = pole if across else first & (m > 0)
+            start(cond, copy(field.at[a:b, 0:2], halo.at[e, b_side, a:b], s_far.at[e, 1, c, 0], r_halo.at[e, b_side, c, 0], b_to))
+
+    def az_copies(e, c, field):
+        a, b, _ = CHUNKS[c]
+        return (
+            copy(field.at[a:b, :, 0:2], hk.at[e, a:b, :, 0:2], s_az.at[e, 0, c], r_az.at[e, 0, c], (mn, az_dn)),
+            copy(field.at[a:b, :, 6:8], hk.at[e, a:b, :, 6:8], s_az.at[e, 1, c], r_az.at[e, 1, c], (mn, az_up)),
+        )
 
     def send_az(e, c, field):
-        a, b, _ = CHUNKS[c]
-        start(None, copy(field.at[a:b, :, 0:2], hk.at[e, a:b, :, 0:2], s_az.at[e, 0, c], r_az.at[e, 0, c], (mn, az_dn)))
-        start(None, copy(field.at[a:b, :, 6:8], hk.at[e, a:b, :, 6:8], s_az.at[e, 1, c], r_az.at[e, 1, c], (mn, az_up)))
+        for one in az_copies(e, c, field):
+            start(None, one)
 
     def send_near(e, c, field):
         a, b, _ = CHUNKS[c]
@@ -143,18 +171,21 @@
         else:
             pl.when(cond)(lambda: c.wait_recv())
 
-    def relay(e, c):
+    def relay(e, c, across):
         _, _, parts = CHUNKS[c]
-        for p in range(4):
-            a, b = parts[p]
-            if p != 3:
-                cond = (x == p) & (m < groups - 1)
+        for p, (a, b) in enumerate(parts):
+            if p != 3 and not across:
+                cond = (x == p) & above
                 await_copy(cond, rf.at[e, a:b], r_rel.at[e, 0, c])
                 start(cond, copy(rf.at[e, a:b], halo.at[e, 0, a:b], s_rel.at[e, 0, c], r_halo.at[e, 0, c, p], f_to))
-            if p != 0:
-                cond = x == p
+            if p != 0 and not (across and c in POLE_CHUNKS):
+                cond = (x == p) & (g0 if across else m > 0)
                 await_copy(cond, rb.at[e, a:b], r_rel.at[e, 1, c])
                 start(cond, copy(rb.at[e, a:b], halo.at[e, b_side, a:b], s_rel.at[e, 1, c], r_halo.at[e, b_side, c, p], b_to))
+            if across and c in POLE_CHUNKS:
+                cond = (x == p) & g6
+                await_copy(cond, rp.at[e, a:b], r_rel.at[e, 2, c])
+                start(cond, copy(rp.at[e, a:b], halo.at[e, 0, a:b], s_rel.at[e, 2, c], r_halo.at[e, 0, c, p], (0, opp)))
 
     def await_margins(e, c):
         a, b, parts = CHUNKS[c]
@@ -263,23 +294,52 @@
                 one(n)
 
     for c in range(NC):
-        send_far(0, c, q)
-    for c in range(NC):
-        send_az(0, c, q)
+        send_to_relays(0, c, q)
+    for c in range(NC):
+        down, up = az_copies(0, c, q)
+        start(az > 0, down)
+        start(None, up)
     for c in range(NC):
         send_near(0, c, q)
-    for c in range(NC):
-        relay(0, c)
+    source(q, s1)
+
+    @pl.when((g0 | g6) & low_z)
+    def _():
+        pl.semaphore_wait(pole_sem, 1)
+
+    for c in range(NC):
+        send_direct(0, c, q, True)
+    for c in range(NC):
+        relay(0, c, True)
+
+    @pl.when(az == 0)
+    def _():
+        pl.semaphore_wait(wrap_sem, 1)
+
+    for c in range(NC):
+        start(az == 0, az_copies(0, c, q)[0])
+
+    @pl.when(even)
+    def _():
+        pl.semaphore_wait(far_sem, 1 + as_int(m > 0))
+
+    for c in range(NC):
+        send_direct(0, c, q, False)
+    for c in range(NC):
+        relay(0, c, False)
     for c in range(NC):
         a, b, _ = CHUNKS[c]
         await_margins(0, c)
         if c == 0:
             coefficients()
         section(0, q, s1, a, b, c > 0, False)
-        send_far(1, c, s1)
+        send_to_relays(1, c, s1)
+        send_direct(1, c, s1, True)
+        send_direct(1, c, s1, False)
         send_az(1, c, s1)
         send_near(1, c, s1)
-        relay(1, c)
+        relay(1, c, True)
+        relay(1, c, False)
     source(s1, new)
     stores = []
     for c in range(NC):
@@ -314,9 +374,10 @@
         out_specs=pl.BlockSpec(memory_space=pl.ANY),
         scratch_shapes=[
             vmem(*block), vmem(*block), vmem(*block), vmem(13, ROWS, ROWS, LANES),
-            vmem(2, 2, *margin), vmem(2, *block), vmem(2, *margin), vmem(2, *margin),
-            pltpu.SemaphoreType.DMA, sems(NC), sems(2, 2, NC, 4), sems(2, 2, NC), sems(2, 2, NC), sems(2, 2, NC),
-            sems(2, 2, NC, 4), sems(2, 2, NC), sems(2, 2, NC),
+            vmem(2, 2, *margin), vmem(2, *block), vmem(2, *margin), vmem(2, *margin), vmem(2, *margin),
+            pltpu.SemaphoreType.DMA, sems(NC), sems(2, 3, NC, 4), sems(2, 2, NC), sems(2, 2, NC), sems(2, 3, NC),
+            sems(2, 2, NC, 4), sems(2, 3, NC), sems(2, 2, NC),
+            pltpu.SemaphoreType.REGULAR, pltpu.SemaphoreType.REGULAR, pltpu.SemaphoreType.REGULAR,
         ],
         compiler_params=pltpu.CompilerParams(
             collective_id=0, has_side_effects=True, vmem_limit_bytes=40 * 1024 * 1024

time: 94.7 us -> 80.7 us (0.85)
  the two profiles are of different devices: /device:TPU:2 before, /device:TPU:96 now
where the time goes in v3:
time: 80.7 us; the launch traced here: 80.5 us
  Pallas kernels  77.4 us (96%)
  local copies, waits for them, and re-layouts  3.11 us (4%)
    pallas_call x1, Pallas kernels, on_device(): pl.pallas_call(kernel, out_shape=jax.ShapeDtypeStruct(block, jnp.float32)...  77.4 us
    unnamed x5, local copies, waits for them, and re-layouts  3.11 us

profile of v3, /device:TPU:96, one launch (start us, length us, event | category | flops | bytes accessed | tf_op | source)
XLA Modules:
  0.0 80.5 jit_solution(17786811225819252710)
XLA Ops:
  0.0 0.0 copy-start
  0.0 1.3 %copy-done = f32[41,8,8,128]{3,2,1,0:T(8,128)S(1)} copy-done((f32[41,8,8,128]{3,2,1,0:T(8,128)S(1)}, f32[41,8,8,128]{3,2,1,0:T(8,128)}, u32[]{:S(2)}) %copy-start) | copy-done | bytes 1343512
  1.3 0.0 copy-start.1
  1.3 0.7 copy-done.1
  2.0 77.4 %shard_map.28 = f32[41,8,8,128]{3,2,1,0:T(8,128)S(1)} custom-call(f32[41,8,8,128]{3,2,1,0:T(8,128)S(1)} %copy-done, f32[30,30]{1,0:T(8,128)S(1)} %copy-done.1), custom_call_target="tpu_custom_call" | custom-call | tf_op jit(solution)/shard_map/pallas_call | solution.py:370
  79.4 1.1 %copy.4 = f32[41,8,8,128]{3,2,1,0:T(8,128)} copy(f32[41,8,8,128]{3,2,1,0:T(8,128)S(1)} %shard_map.28) | data formatting | bytes 2686976
Async XLA Ops:
  0.0 1.3 %copy-start = (f32[41,8,8,128]{3,2,1,0:T(8,128)S(1)}, f32[41,8,8,128]{3,2,1,0:T(8,128)}, u32[]{:S(2)}) copy-start(f32[41,8,8,128]{3,2,1,0:T(8,128)} %flow.1) | copy-start | bytes 4030468
  1.3 0.7 copy-start.1

commit v4 on v3

--- a/solution.py
+++ b/solution.py
@@ -14,18 +14,19 @@
 NQ, NLEV, FIRST_LEVEL, ELECTRON = 41, 30, 11, 10
 ROWS, LANES = 8, 128
 COLUMNS = 4
-BOUNDS = (0, 11, 21, 31, 41)
-UNROLL = 10
-POLE_GROUP, POLE_CHUNKS = 6, (1, 3)
-
-
-def parts_of(a, b):
-    cuts = [a + ((b - a) * p + COLUMNS - 1) // COLUMNS for p in range(COLUMNS + 1)]
-    return [(cuts[p], cuts[p + 1]) for p in range(COLUMNS)]
-
-
-CHUNKS = [(a, b, parts_of(a, b)) for a, b in zip(BOUNDS[:-1], BOUNDS[1:])]
-NC = len(CHUNKS)
+VMEM_LIMIT = 40 * 1024 * 1024
+SIZES = ((3, 3, 3, 2), (4, 3, 4, 4), (3, 4, 4, 4))
+LAG = 1
+POLE_GROUP, POLE_CHUNKS = 6, (0, 2)
+
+
+def cuts(start, sizes):
+    bounds = [start + sum(sizes[:p]) for p in range(COLUMNS + 1)]
+    return bounds[0], bounds[-1], list(zip(bounds[:-1], bounds[1:]))
+
+
+NC = len(SIZES)
+CHUNKS = [cuts(sum(sum(sizes) for sizes in SIZES[:c]), SIZES[c]) for c in range(NC)]
 
 
 def as_int(flag):
@@ -51,6 +52,13 @@
     g0, g6 = m == 0, m == POLE_GROUP
     low_z, high_z = az < n_az // 2, az >= n_az // 2
     above = m < groups - 1
+    not_first, not_last = jnp.logical_not(first), jnp.logical_not(last)
+    back, back_or_pole = first & (m > 0), first
+    wrap_dn, no_wrap_dn = az == 0, az > 0
+    relays_f = [(x == p) & above for p in range(4)]
+    relays_b = [(x == p) & (m > 0) for p in range(4)]
+    relays_0 = [(x == p) & g0 for p in range(4)]
+    relays_6 = [(x == p) & g6 for p in range(4)]
     bar = pltpu.get_barrier_semaphore()
 
     def tell(cond, device, sem=bar):
@@ -120,23 +128,27 @@
     def copy(src, dst, s, r, device):
         return pltpu.make_async_remote_copy(src, dst, s, r, device_id=device, device_id_type=MESH)
 
-    def start(cond, c):
+    def start(cond, *copies):
+        def go():
+            for c in copies:
+                c.start()
         if cond is None:
-            c.start()
+            go()
         else:
-            pl.when(cond)(lambda: c.start())
-        started.append((cond, c))
+            pl.when(cond)(go)
+        started.append((cond, copies))
 
     def send_to_relays(e, c, field):
         _, _, parts = CHUNKS[c]
-        for p, (a, b) in enumerate(parts):
-            if p != 3:
-                start(up_far, copy(field.at[a:b, 6:8], rf.at[e, a:b], s_far.at[e, 0, c, p], r_rel.at[e, 0, c], (4 * m + p, az)))
-            if p != 0:
-                cond = first & (m > 0) if c in POLE_CHUNKS else first
-                start(cond, copy(field.at[a:b, 0:2], rb.at[e, a:b], s_far.at[e, 1, c, p], r_rel.at[e, 1, c], (4 * m + p, az)))
-            if c in POLE_CHUNKS:
-                start(pole, copy(field.at[a:b, 0:2], rp.at[e, a:b], s_far.at[e, 2, c, p], r_rel.at[e, 2, c], (4 * POLE_GROUP + p, az)))
+
+        def handed(side, rows, to, p, group):
+            a, b = parts[p]
+            return copy(field.at[a:b, rows:rows + 2], to.at[e, a:b], s_far.at[e, side, c, p], r_rel.at[e, side, c], (4 * group + p, az))
+
+        start(up_far, *[handed(0, 6, rf, p, m) for p in range(3)])
+        start(back if c in POLE_CHUNKS else back_or_pole, *[handed(1, 0, rb, p, m) for p in range(1, 4)])
+        if c in POLE_CHUNKS:
+            start(pole, *[handed(2, 0, rp, p, POLE_GROUP) for p in range(4)])
 
     def send_direct(e, c, field, across):
         _, _, parts = CHUNKS[c]
@@ -145,7 +157,7 @@
             start(up_far, copy(field.at[a:b, 6:8], halo.at[e, 0, a:b], s_far.at[e, 0, c, 3], r_halo.at[e, 0, c, 3], f_to))
         a, b = parts[0]
         if not across or c not in POLE_CHUNKS:
-            cond = pole if across else first & (m > 0)
+            cond = pole if across else back
             start(cond, copy(field.at[a:b, 0:2], halo.at[e, b_side, a:b], s_far.at[e, 1, c, 0], r_halo.at[e, b_side, c, 0], b_to))
 
     def az_copies(e, c, field):
@@ -156,47 +168,45 @@
         )
 
     def send_az(e, c, field):
-        for one in az_copies(e, c, field):
-            start(None, one)
+        start(None, *az_copies(e, c, field))
 
     def send_near(e, c, field):
         a, b, _ = CHUNKS[c]
-        start(jnp.logical_not(last), copy(field.at[a:b, 6:8], halo.at[e, 0, a:b], s_near.at[e, 0, c], r_halo.at[e, 0, c, 0], (mn + 1, az)))
-        start(jnp.logical_not(first), copy(field.at[a:b, 0:2], halo.at[e, 1, a:b], s_near.at[e, 1, c], r_halo.at[e, 1, c, 0], (mn - 1, az)))
-
-    def await_copy(cond, dst, r):
-        c = copy(dst, dst, in_sem, r, f_to)
+        start(not_last, copy(field.at[a:b, 6:8], halo.at[e, 0, a:b], s_near.at[e, 0, c], r_halo.at[e, 0, c, 0], (mn + 1, az)))
+        start(not_first, copy(field.at[a:b, 0:2], halo.at[e, 1, a:b], s_near.at[e, 1, c], r_halo.at[e, 1, c, 0], (mn - 1, az)))
+
+    def await_copies(cond, *landed):
+        def go():
+            for dst, r in landed:
+                copy(dst, dst, in_sem, r, f_to).wait_recv()
         if cond is None:
-            c.wait_recv()
+            go()
         else:
-            pl.when(cond)(lambda: c.wait_recv())
+            pl.when(cond)(go)
 
     def relay(e, c, across):
         _, _, parts = CHUNKS[c]
-        for p, (a, b) in enumerate(parts):
+
+        def passed_on(cond, held, side, to, p, device):
+            a, b = parts[p]
+            await_copies(cond, (held.at[e, a:b], r_rel.at[e, side, c]))
+            start(cond, copy(held.at[e, a:b], halo.at[e, to, a:b], s_rel.at[e, side, c], r_halo.at[e, to, c, p], device))
+
+        for p in range(4):
             if p != 3 and not across:
-                cond = (x == p) & above
-                await_copy(cond, rf.at[e, a:b], r_rel.at[e, 0, c])
-                start(cond, copy(rf.at[e, a:b], halo.at[e, 0, a:b], s_rel.at[e, 0, c], r_halo.at[e, 0, c, p], f_to))
+                passed_on(relays_f[p], rf, 0, 0, p, f_to)
             if p != 0 and not (across and c in POLE_CHUNKS):
-                cond = (x == p) & (g0 if across else m > 0)
-                await_copy(cond, rb.at[e, a:b], r_rel.at[e, 1, c])
-                start(cond, copy(rb.at[e, a:b], halo.at[e, b_side, a:b], s_rel.at[e, 1, c], r_halo.at[e, b_side, c, p], b_to))
+                passed_on((relays_0 if across else relays_b)[p], rb, 1, b_side, p, b_to)
             if across and c in POLE_CHUNKS:
-                cond = (x == p) & g6
-                await_copy(cond, rp.at[e, a:b], r_rel.at[e, 2, c])
-                start(cond, copy(rp.at[e, a:b], halo.at[e, 0, a:b], s_rel.at[e, 2, c], r_halo.at[e, 0, c, p], (0, opp)))
+                passed_on(relays_6[p], rp, 2, 0, p, (0, opp))
 
     def await_margins(e, c):
         a, b, parts = CHUNKS[c]
-        await_copy(None, hk.at[e, a:b, :, 0:2], r_az.at[e, 0, c])
-        await_copy(None, hk.at[e, a:b, :, 6:8], r_az.at[e, 1, c])
-        await_copy(jnp.logical_not(first), halo.at[e, 0, a:b], r_halo.at[e, 0, c, 0])
-        await_copy(jnp.logical_not(last), halo.at[e, 1, a:b], r_halo.at[e, 1, c, 0])
-        for p in range(4):
-            pa, pb = parts[p]
-            await_copy(first, halo.at[e, 0, pa:pb], r_halo.at[e, 0, c, p])
-            await_copy(up_far, halo.at[e, 1, pa:pb], r_halo.at[e, 1, c, p])
+        await_copies(None, (hk.at[e, a:b, :, 0:2], r_az.at[e, 0, c]), (hk.at[e, a:b, :, 6:8], r_az.at[e, 1, c]))
+        await_copies(not_first, (halo.at[e, 0, a:b], r_halo.at[e, 0, c, 0]))
+        await_copies(not_last, (halo.at[e, 1, a:b], r_halo.at[e, 1, c, 0]))
+        for cond, side in ((first, 0), (up_far, 1)):
+            await_copies(cond, *[(halo.at[e, side, pa:pb], r_halo.at[e, side, c, p]) for p, (pa, pb) in enumerate(parts)])
         if c == 0:
             @pl.when(pole)
             def _():
@@ -282,22 +292,16 @@
                 r = (sums[0] + sums[1]) + (sums[2] + sums[3])
                 if chemistry:
                     r = r + acc[n, i]
-                acc[n, i] = 0.5 * (q[n, i] + r) if final else r
-
-            def several(g, _):
-                for s in range(UNROLL):
-                    one(a + g * UNROLL + s)
-                return 0
-
-            lax.fori_loop(0, (b - a) // UNROLL, several, 0)
-            for n in range(a + (b - a) // UNROLL * UNROLL, b):
+                acc[n, i] = 0.5 * r if final else r
+
+            for n in range(a, b):
                 one(n)
 
     for c in range(NC):
         send_to_relays(0, c, q)
     for c in range(NC):
         down, up = az_copies(0, c, q)
-        start(az > 0, down)
+        start(no_wrap_dn, down)
         start(None, up)
     for c in range(NC):
         send_near(0, c, q)
@@ -317,7 +321,7 @@
         pl.semaphore_wait(wrap_sem, 1)
 
     for c in range(NC):
-        start(az == 0, az_copies(0, c, q)[0])
+        start(wrap_dn, az_copies(0, c, q)[0])
 
     @pl.when(even)
     def _():
@@ -338,6 +342,10 @@
         send_direct(1, c, s1, False)
         send_az(1, c, s1)
         send_near(1, c, s1)
+        if c >= LAG:
+            relay(1, c - LAG, True)
+            relay(1, c - LAG, False)
+    for c in range(NC - LAG, NC):
         relay(1, c, True)
         relay(1, c, False)
     source(s1, new)
@@ -349,11 +357,17 @@
         store = pltpu.make_async_copy(new.at[a:b], out.at[a:b], out_sem.at[c])
         store.start()
         stores.append(store)
-    for cond, c in started:
+    groups_of = {}
+    for cond, copies in started:
+        groups_of.setdefault(id(cond), (cond, []))[1].extend(copies)
+    for cond, copies in groups_of.values():
+        def go(copies=copies):
+            for c in copies:
+                c.wait_send()
         if cond is None:
-            c.wait_send()
+            go()
         else:
-            pl.when(cond)(lambda c=c: c.wait_send())
+            pl.when(cond)(go)
     for store in stores:
         store.wait()
 
@@ -367,7 +381,7 @@
 
     block = (NQ, ROWS, ROWS, LANES)
     margin = (NQ, 2, ROWS, LANES)
-    return pl.pallas_call(
+    half = pl.pallas_call(
         kernel,
         out_shape=jax.ShapeDtypeStruct(block, jnp.float32),
         in_specs=[pl.BlockSpec(memory_space=pl.ANY), pl.BlockSpec(memory_space=pltpu.SMEM)],
@@ -380,9 +394,10 @@
             pltpu.SemaphoreType.REGULAR, pltpu.SemaphoreType.REGULAR, pltpu.SemaphoreType.REGULAR,
         ],
         compiler_params=pltpu.CompilerParams(
-            collective_id=0, has_side_effects=True, vmem_limit_bytes=40 * 1024 * 1024
+            collective_id=0, has_side_effects=True, vmem_limit_bytes=VMEM_LIMIT
         ),
     )(flow_state, level_rates)
+    return 0.5 * flow_state + half
 
 
 def solution(mesh):

time: 80.7 us -> 72.8 us (0.902)
  Pallas kernels: 77.4 us -> 69.2 us
  other arithmetic: 0 us -> 1.3 us
  local copies, waits for them, and re-layouts: 3.11 us -> 2.04 us
    pallas_call x1, Pallas kernels: 77.4 us -> 69.2 us  [on_device(): pl.pallas_call(kernel, out_shape=jax.ShapeDtypeStruct(block, jnp.float32)...]
    add x0 -> x1, other arithmetic: none -> 1.3 us  [on_device(): return 0.5 * flow_state + half]
    unnamed x5 -> x4, local copies, waits for them, and re-layouts: 3.11 us -> 2.04 us
where the time goes in v4:
time: 72.8 us; the launch traced here: 72.6 us
  Pallas kernels  69.2 us (95%)
  local copies, waits for them, and re-layouts  2.04 us (3%)
  other arithmetic  1.3 us (2%)
    pallas_call x1, Pallas kernels, on_device(): pl.pallas_call(kernel, out_shape=jax.ShapeDtypeStruct(block, jnp.float32)...  69.2 us
    unnamed x4, local copies, waits for them, and re-layouts  2.04 us

profile of v4, /device:TPU:96, one launch (start us, length us, event | category | flops | bytes accessed | tf_op | source)
XLA Modules:
  0.0 72.6 jit_solution(17213467435835782596)
XLA Ops:
  0.0 0.0 copy-start
  0.0 1.3 %copy-done = f32[41,8,8,128]{3,2,1,0:T(8,128)S(1)} copy-done((f32[41,8,8,128]{3,2,1,0:T(8,128)S(1)}, f32[41,8,8,128]{3,2,1,0:T(8,128)}, u32[]{:S(2)}) %copy-start) | copy-done | bytes 1343512
  1.3 0.0 copy-start.1
  1.3 0.7 copy-done.1
  2.0 69.2 %shard_map.28 = f32[41,8,8,128]{3,2,1,0:T(8,128)S(1)} custom-call(f32[41,8,8,128]{3,2,1,0:T(8,128)S(1)} %copy-done, f32[30,30]{1,0:T(8,128)S(1)} %copy-done.1), custom_call_target="tpu_custom_call" | custom-call | tf_op jit(solution)/shard_map/pallas_call | solution.py:384
  71.3 1.3 %multiply_add_fusion = f32[41,8,8,128]{3,2,1,0:T(8,128)} fusion(f32[41,8,8,128]{3,2,1,0:T(8,128)S(1)} %shard_map.28, f32[41,8,8,128]{3,2,1,0:T(8,128)S(1)} %copy-done), kind=kLoop, calls=%fused_computation | loop fusion | flops 671744 | bytes 4030464 | tf_op jit(solution)/shard_map/add | solution.py:400
Async XLA Ops:
  0.0 1.3 %copy-start = (f32[41,8,8,128]{3,2,1,0:T(8,128)S(1)}, f32[41,8,8,128]{3,2,1,0:T(8,128)}, u32[]{:S(2)}) copy-start(f32[41,8,8,128]{3,2,1,0:T(8,128)} %flow.1) | copy-start | bytes 4030468
  1.3 0.7 copy-start.1

commit v5 on v4

--- a/solution.py
+++ b/solution.py
@@ -14,8 +14,9 @@
 NQ, NLEV, FIRST_LEVEL, ELECTRON = 41, 30, 11, 10
 ROWS, LANES = 8, 128
 COLUMNS = 4
-VMEM_LIMIT = 40 * 1024 * 1024
-SIZES = ((3, 3, 3, 2), (4, 3, 4, 4), (3, 4, 4, 4))
+VMEM_LIMIT = 60 * 1024 * 1024
+UP_SIZES = ((3, 3, 3, 2), (4, 3, 4, 4), (3, 4, 4, 4))
+DOWN_SIZES = ((3, 3, 3, 2), (3, 4, 4, 4), (4, 4, 3, 4))
 LAG = 1
 POLE_GROUP, POLE_CHUNKS = 6, (0, 2)
 
@@ -25,8 +26,9 @@
     return bounds[0], bounds[-1], list(zip(bounds[:-1], bounds[1:]))
 
 
-NC = len(SIZES)
-CHUNKS = [cuts(sum(sum(sizes) for sizes in SIZES[:c]), SIZES[c]) for c in range(NC)]
+NC = len(UP_SIZES)
+STARTS = [sum(sum(sizes) for sizes in UP_SIZES[:c]) for c in range(NC)]
+CHUNKS = [(*cuts(STARTS[c], UP_SIZES[c]), cuts(STARTS[c], DOWN_SIZES[c])[2]) for c in range(NC)]
 
 
 def as_int(flag):
@@ -95,7 +97,6 @@
         for e in range(2):
             halo[e, 1] = jnp.zeros((NQ, 2, ROWS, LANES), jnp.float32)
 
-    load.wait()
 
     def source(field, acc):
         def pair(t, _):
@@ -139,10 +140,10 @@
         started.append((cond, copies))
 
     def send_to_relays(e, c, field):
-        _, _, parts = CHUNKS[c]
+        _, _, ups, downs = CHUNKS[c]
 
         def handed(side, rows, to, p, group):
-            a, b = parts[p]
+            a, b = (downs if side else ups)[p]
             return copy(field.at[a:b, rows:rows + 2], to.at[e, a:b], s_far.at[e, side, c, p], r_rel.at[e, side, c], (4 * group + p, az))
 
         start(up_far, *[handed(0, 6, rf, p, m) for p in range(3)])
@@ -151,17 +152,17 @@
             start(pole, *[handed(2, 0, rp, p, POLE_GROUP) for p in range(4)])
 
     def send_direct(e, c, field, across):
-        _, _, parts = CHUNKS[c]
-        a, b = parts[3]
+        _, _, ups, downs = CHUNKS[c]
+        a, b = ups[3]
         if not across:
             start(up_far, copy(field.at[a:b, 6:8], halo.at[e, 0, a:b], s_far.at[e, 0, c, 3], r_halo.at[e, 0, c, 3], f_to))
-        a, b = parts[0]
+        a, b = downs[0]
         if not across or c not in POLE_CHUNKS:
             cond = pole if across else back
             start(cond, copy(field.at[a:b, 0:2], halo.at[e, b_side, a:b], s_far.at[e, 1, c, 0], r_halo.at[e, b_side, c, 0], b_to))
 
     def az_copies(e, c, field):
-        a, b, _ = CHUNKS[c]
+        a, b, _, _ = CHUNKS[c]
         return (
             copy(field.at[a:b, :, 0:2], hk.at[e, a:b, :, 0:2], s_az.at[e, 0, c], r_az.at[e, 0, c], (mn, az_dn)),
             copy(field.at[a:b, :, 6:8], hk.at[e, a:b, :, 6:8], s_az.at[e, 1, c], r_az.at[e, 1, c], (mn, az_up)),
@@ -171,7 +172,7 @@
         start(None, *az_copies(e, c, field))
 
     def send_near(e, c, field):
-        a, b, _ = CHUNKS[c]
+        a, b, _, _ = CHUNKS[c]
         start(not_last, copy(field.at[a:b, 6:8], halo.at[e, 0, a:b], s_near.at[e, 0, c], r_halo.at[e, 0, c, 0], (mn + 1, az)))
         start(not_first, copy(field.at[a:b, 0:2], halo.at[e, 1, a:b], s_near.at[e, 1, c], r_halo.at[e, 1, c, 0], (mn - 1, az)))
 
@@ -185,10 +186,10 @@
             pl.when(cond)(go)
 
     def relay(e, c, across):
-        _, _, parts = CHUNKS[c]
+        _, _, ups, downs = CHUNKS[c]
 
         def passed_on(cond, held, side, to, p, device):
-            a, b = parts[p]
+            a, b = (downs if side else ups)[p]
             await_copies(cond, (held.at[e, a:b], r_rel.at[e, side, c]))
             start(cond, copy(held.at[e, a:b], halo.at[e, to, a:b], s_rel.at[e, side, c], r_halo.at[e, to, c, p], device))
 
@@ -201,11 +202,11 @@
                 passed_on(relays_6[p], rp, 2, 0, p, (0, opp))
 
     def await_margins(e, c):
-        a, b, parts = CHUNKS[c]
+        a, b, ups, downs = CHUNKS[c]
         await_copies(None, (hk.at[e, a:b, :, 0:2], r_az.at[e, 0, c]), (hk.at[e, a:b, :, 6:8], r_az.at[e, 1, c]))
         await_copies(not_first, (halo.at[e, 0, a:b], r_halo.at[e, 0, c, 0]))
         await_copies(not_last, (halo.at[e, 1, a:b], r_halo.at[e, 1, c, 0]))
-        for cond, side in ((first, 0), (up_far, 1)):
+        for cond, side, parts in ((back, 0, ups), (pole, 0, downs), (up_far, 1, downs)):
             await_copies(cond, *[(halo.at[e, side, pa:pb], r_halo.at[e, side, c, p]) for p, (pa, pb) in enumerate(parts)])
         if c == 0:
             @pl.when(pole)
@@ -297,6 +298,7 @@
             for n in range(a, b):
                 one(n)
 
+    load.wait()
     for c in range(NC):
         send_to_relays(0, c, q)
     for c in range(NC):
@@ -332,7 +334,7 @@
     for c in range(NC):
         relay(0, c, False)
     for c in range(NC):
-        a, b, _ = CHUNKS[c]
+        a, b, _, _ = CHUNKS[c]
         await_margins(0, c)
         if c == 0:
             coefficients()
@@ -351,7 +353,7 @@
     source(s1, new)
     stores = []
     for c in range(NC):
-        a, b, _ = CHUNKS[c]
+        a, b, _, _ = CHUNKS[c]
         await_margins(1, c)
         section(1, s1, new, a, b, c > 0, True)
         store = pltpu.make_async_copy(new.at[a:b], out.at[a:b], out_sem.at[c])

time: 72.8 us -> 72.2 us (level)
  the two profiles are of different devices: /device:TPU:96 before, /device:TPU:151 now
where the time goes in v5:
time: 72.2 us; the launch traced here: 72 us
  Pallas kernels  69.2 us (96%)
  other arithmetic  2.72 us (4%)
    pallas_call x1, Pallas kernels, on_device(): pl.pallas_call(kernel, out_shape=jax.ShapeDtypeStruct(block, jnp.float32)...  69.2 us
    add x1, other arithmetic, on_device(): return 0.5 * flow_state + half  2.72 us

profile of v5, /device:TPU:151, one launch (start us, length us, event | category | flops | bytes accessed | tf_op | source)
XLA Modules:
  0.0 72.0 jit_solution(8337601037094506556)
XLA Ops:
  0.0 0.0 copy-start
  0.0 69.2 %shard_map.28 = f32[41,8,8,128]{3,2,1,0:T(8,128)} custom-call(f32[41,8,8,128]{3,2,1,0:T(8,128)} %flow.1, f32[30,30]{1,0:T(8,128)} %rates.1), custom_call_target="tpu_custom_call" | custom-call | tf_op jit(solution)/shard_map/pallas_call | solution.py:386
  69.2 0.0 copy-done
  69.2 2.7 %multiply_add_fusion = f32[41,8,8,128]{3,2,1,0:T(8,128)} fusion(f32[41,8,8,128]{3,2,1,0:T(8,128)} %shard_map.28, f32[41,8,8,128]{3,2,1,0:T(8,128)S(1)} %copy-done), kind=kLoop, calls=%fused_computation | loop fusion | flops 671744 | bytes 4030464 | tf_op jit(solution)/shard_map/add | solution.py:402
Async XLA Ops:
  0.0 69.2 %copy-start = (f32[41,8,8,128]{3,2,1,0:T(8,128)S(1)}, f32[41,8,8,128]{3,2,1,0:T(8,128)}, u32[]{:S(2)}) copy-start(f32[41,8,8,128]{3,2,1,0:T(8,128)} %flow.1) | copy-start | bytes 4030468

commit v6 on v5

--- a/solution.py
+++ b/solution.py
@@ -18,6 +18,7 @@
 UP_SIZES = ((3, 3, 3, 2), (4, 3, 4, 4), (3, 4, 4, 4))
 DOWN_SIZES = ((3, 3, 3, 2), (3, 4, 4, 4), (4, 4, 3, 4))
 LAG = 1
+INNER, OUTER = (2, 3, 4, 5), (0, 1, 6, 7)
 POLE_GROUP, POLE_CHUNKS = 6, (0, 2)
 
 
@@ -201,11 +202,14 @@
             if across and c in POLE_CHUNKS:
                 passed_on(relays_6[p], rp, 2, 0, p, (0, opp))
 
-    def await_margins(e, c):
-        a, b, ups, downs = CHUNKS[c]
+    def await_near(e, c):
+        a, b, _, _ = CHUNKS[c]
         await_copies(None, (hk.at[e, a:b, :, 0:2], r_az.at[e, 0, c]), (hk.at[e, a:b, :, 6:8], r_az.at[e, 1, c]))
         await_copies(not_first, (halo.at[e, 0, a:b], r_halo.at[e, 0, c, 0]))
         await_copies(not_last, (halo.at[e, 1, a:b], r_halo.at[e, 1, c, 0]))
+
+    def await_far(e, c):
+        _, _, ups, downs = CHUNKS[c]
         for cond, side, parts in ((back, 0, ups), (pole, 0, downs), (up_far, 1, downs)):
             await_copies(cond, *[(halo.at[e, side, pa:pb], r_halo.at[e, side, c, p]) for p, (pa, pb) in enumerate(parts)])
         if c == 0:
@@ -247,19 +251,16 @@
             (3.0 * TIME_STEP) * (s_p + s_m),
         )
 
-    def coefficients():
+    def coefficients(rows):
         def density(read):
             return 1.0 / jnp.maximum(read(0) + read(1) + read(2) + read(3) + read(4), 1.0)
 
         def u_i(i):
             return row(0, q, 5, i) * density(lambda n: row(0, q, n, i))
 
-        u_m, u = u_i(-1), u_i(0)
-        for i in range(ROWS):
-            u_p = u_i(i + 1)
+        for i in rows:
             inverse = density(lambda n: q[n, i])
-            ti = taps(u_m, u, u_p)
-            u_m, u = u, u_p
+            ti = taps(u_i(i - 1), q[5, i] * inverse, u_i(i + 1))
             uk = q[7, i] * inverse
             hk_u = hk[0, 7, i] * density(lambda n: hk[0, n, i])
             shifted = along_k(uk, hk_u)
@@ -277,17 +278,17 @@
             coef[11, i] = jnp.where(j_at > 1, tj[3], 0.0)
             coef[12, i] = 1.0 + ti[4] + tk[4] + tj[4]
 
-    def section(e, field, acc, a, b, chemistry, final):
-        for i in range(ROWS):
+    def section(e, field, acc, rows, a, b, chemistry, final):
+        for i in rows:
             cs = [coef[t, i] for t in range(13)]
 
             def one(n):
                 v = field[n, i]
                 ks = along_k(v, hk[e, n, i])
                 js = [pltpu.roll(v, (LANES - d) % LANES, 1) for d in (1, 2, -1, -2)]
-                rows = [row(e, field, n, i + d) for d in (1, 2, -1, -2)]
+                along_i = [row(e, field, n, i + d) for d in (1, 2, -1, -2)]
                 sums = [cs[12] * v]
-                for base, values in ((0, rows), (4, ks), (8, js)):
+                for base, values in ((0, along_i), (4, ks), (8, js)):
                     t = [cs[base + d] * values[d] for d in range(4)]
                     sums.append((t[0] + t[1]) + (t[2] + t[3]))
                 r = (sums[0] + sums[1]) + (sums[2] + sums[3])
@@ -335,10 +336,14 @@
         relay(0, c, False)
     for c in range(NC):
         a, b, _, _ = CHUNKS[c]
-        await_margins(0, c)
+        await_near(0, c)
         if c == 0:
-            coefficients()
-        section(0, q, s1, a, b, c > 0, False)
+            coefficients(INNER)
+        section(0, q, s1, INNER, a, b, c > 0, False)
+        await_far(0, c)
+        if c == 0:
+            coefficients(OUTER)
+        section(0, q, s1, OUTER, a, b, c > 0, False)
         send_to_relays(1, c, s1)
         send_direct(1, c, s1, True)
         send_direct(1, c, s1, False)
@@ -354,8 +359,10 @@
     stores = []
     for c in range(NC):
         a, b, _, _ = CHUNKS[c]
-        await_margins(1, c)
-        section(1, s1, new, a, b, c > 0, True)
+        await_near(1, c)
+        section(1, s1, new, INNER, a, b, c > 0, True)
+        await_far(1, c)
+        section(1, s1, new, OUTER, a, b, c > 0, True)
         store = pltpu.make_async_copy(new.at[a:b], out.at[a:b], out_sem.at[c])
         store.start()
         stores.append(store)

time: 72.2 us -> 71.8 us (level)
  no operation moved by 1% of the time
where the time goes in v6:
time: 71.8 us; the launch traced here: 71.6 us
  Pallas kernels  68.9 us (96%)
  other arithmetic  2.72 us (4%)
    pallas_call x1, Pallas kernels, on_device(): pl.pallas_call(kernel, out_shape=jax.ShapeDtypeStruct(block, jnp.float32)...  68.9 us
    add x1, other arithmetic, on_device(): return 0.5 * flow_state + half  2.72 us

profile of v6, /device:TPU:151, one launch (start us, length us, event | category | flops | bytes accessed | tf_op | source)
XLA Modules:
  0.0 71.6 jit_solution(10049460272698139828)
XLA Ops:
  0.0 0.0 copy-start
  0.0 68.9 %shard_map.28 = f32[41,8,8,128]{3,2,1,0:T(8,128)} custom-call(f32[41,8,8,128]{3,2,1,0:T(8,128)} %flow.1, f32[30,30]{1,0:T(8,128)} %rates.1), custom_call_target="tpu_custom_call" | custom-call | tf_op jit(solution)/shard_map/pallas_call | solution.py:393
  68.9 0.0 copy-done
  68.9 2.7 %multiply_add_fusion = f32[41,8,8,128]{3,2,1,0:T(8,128)} fusion(f32[41,8,8,128]{3,2,1,0:T(8,128)} %shard_map.28, f32[41,8,8,128]{3,2,1,0:T(8,128)S(1)} %copy-done), kind=kLoop, calls=%fused_computation | loop fusion | flops 671744 | bytes 4030464 | tf_op jit(solution)/shard_map/add | solution.py:409
Async XLA Ops:
  0.0 68.9 %copy-start = (f32[41,8,8,128]{3,2,1,0:T(8,128)S(1)}, f32[41,8,8,128]{3,2,1,0:T(8,128)}, u32[]{:S(2)}) copy-start(f32[41,8,8,128]{3,2,1,0:T(8,128)} %flow.1) | copy-start | bytes 4030468
